TPU v7x, 32 devices: a whole 2x2x4 slice. The times are simulated.
32 devices in a mesh: rows: 8 (over z, x), filt: 4 (over y, core).
Axes of the slice: x: 2, y: 2, z: 4, core: 2. Of those that a mesh axis runs over, the one named last changes fastest.
Arguments:
- features: bfloat16 [96, 48, 2048], P('rows'), may hold values from -6 to 6
- point_weight: bfloat16 [2048, 256], P(None, 'filt'), may hold values from -0.125 to 0.125
- dilated_weight: bfloat16 [3, 3, 3, 2048, 256], P(None, None, None, None, 'filt'), may hold values from -0.046875 to 0.046875
- branch_bias: float32 [4, 256], P(None, 'filt'), may hold values from -3 to 3
- project_weight: bfloat16 [4, 256, 256], replicated, may hold values from -0.1875 to 0.1875
- project_bias: float32 [256], replicated, may hold values from -3 to 3
- cotangent: bfloat16 [96, 48, 256], P('rows'), may hold values from -6 to 6
Outputs:
- head_output: bfloat16 [96, 48, 256], P('rows', None, 'filt')
- feature_grad: bfloat16 [96, 48, 2048], P('rows', None, 'filt')
All inputs are finite; a program needn't handle non-finite values.
Results may differ from a plain program's by a relative error of at most 0.035.
The roundings to bfloat16 on the way count: a program that leaves them out, or rounds other values in their place, can miss the bound.
Values may be sent and summed in bfloat16 or wider, within the bound.
No kernel may reach another device: no remote copies, remote signals or barrier semaphores. Data moves between devices by JAX's collectives and lax.ppermute only.
A program may use at most 128 MiB of HBM per device.

v0:
```python
import jax
import jax.numpy as jnp
from jax import lax
from jax.sharding import PartitionSpec as P

FIRST_DILATION = 12
SECOND_DILATION = 24
THIRD_DILATION = 36


def passed_along(x, axis, by):
    devices = lax.axis_size(axis)
    pairs = [(i, i + by) for i in range(devices) if 0 <= i + by < devices]
    return lax.ppermute(x, axis, pairs)


def shift_columns(field, amount):
    breadth = field.shape[1]
    if amount == 0:
        return field
    padding = [(0, 0)] * field.ndim
    if amount > 0:
        kept = field[:, amount:]
        padding[1] = (0, amount)
    else:
        kept = field[:, : breadth + amount]
        padding[1] = (-amount, 0)
    return jnp.pad(kept, padding)


def fetch_sums(field, offset):
    return passed_along(field, "rows", offset)


def fetch_grads(field, offset):
    return passed_along(field, "rows", offset)


def shift_rows(field, amount, fetcher):
    height = field.shape[0]
    quotient = amount // height

    def extract_block(offset):
        if offset == 0:
            return field
        return fetcher(field, offset)

    return extract_block(quotient)


def make_kernel_taps(variants, dilation_rates):
    stacked = [variants[:, :, 0]]
    for branch, dilation in enumerate(dilation_rates):
        for row_tap in range(3):
            source = variants[:, :, 1 + 3 * branch + row_tap]
            for col_tap in range(3):
                stacked.append(shift_columns(source, -(col_tap - 1) * dilation))
    return jnp.stack(stacked, 2)


def on_device(
    features, point_weight, dilated_weight, branch_bias, project_weight, project_bias, cotangent
):
    height, breadth, channels = features.shape
    pixels = height * breadth
    own_width = point_weight.shape[1]
    filters = lax.axis_size("filt")
    member = lax.axis_index("filt")
    branch_outputs = project_weight.shape[2]
    own_out = branch_outputs // filters
    own_channels = channels // filters
    dilation_rates = (FIRST_DILATION, SECOND_DILATION, THIRD_DILATION)
    all_weights = jnp.concatenate(
        [point_weight[None], dilated_weight.reshape(27, channels, own_width)], 0
    )
    flattened = features.reshape(pixels, channels)
    tap_terms = jnp.einsum(
        "pc,tco->pto", flattened, all_weights, preferred_element_type=jnp.float32
    )
    tap_terms = tap_terms.reshape(height, breadth, 28, own_width)
    pre_list = [tap_terms[:, :, 0, :] + branch_bias[0]]
    for branch, dilation in enumerate(dilation_rates):
        summed_result = jnp.zeros((height, breadth, own_width), jnp.float32)
        for row_tap in range(3):
            row_sum = jnp.zeros((height, breadth, own_width), jnp.float32)
            for col_tap in range(3):
                row_sum = row_sum + shift_columns(
                    tap_terms[:, :, 1 + 9 * branch + 3 * row_tap + col_tap, :],
                    (col_tap - 1) * dilation,
                )
            summed_result = summed_result + shift_rows(
                row_sum, -(row_tap - 1) * dilation, fetch_sums
            )
        pre_list.append(summed_result + branch_bias[branch + 1])
    branch_pre = jnp.stack(pre_list, 2)
    activations = jnp.maximum(branch_pre, 0.0).astype(jnp.bfloat16).reshape(pixels, 4 * own_width)
    grouped = project_weight.reshape(4, filters, own_width, branch_outputs)
    own_rows = lax.dynamic_index_in_dim(grouped, member, 1, keepdims=False).reshape(
        4 * own_width, branch_outputs
    )
    flat_cotangent = cotangent.reshape(pixels, branch_outputs)
    ordered = jnp.transpose(grouped, (1, 0, 2, 3)).reshape(filters * 4 * own_width, branch_outputs)
    project_pre = jnp.dot(
        lax.all_gather(activations, "filt", axis=1, tiled=True),
        ordered,
        preferred_element_type=jnp.float32,
    )
    project_pre = project_pre + project_bias
    head_grad = jnp.where(project_pre > 0, flat_cotangent.astype(jnp.float32), 0.0).astype(
        jnp.bfloat16
    )
    own_pre = lax.dynamic_slice_in_dim(project_pre, member * own_out, own_out, 1)
    act_grad = jnp.dot(head_grad, own_rows.T, preferred_element_type=jnp.float32)
    head_output = jnp.maximum(own_pre, 0.0).astype(jnp.bfloat16).reshape(height, breadth, own_out)
    branch_grad = jnp.where(
        branch_pre > 0, act_grad.reshape(height, breadth, 4, own_width), 0.0
    ).astype(jnp.bfloat16)
    variant_list = [branch_grad[:, :, 0, :]]
    for branch, dilation in enumerate(dilation_rates):
        for row_tap in range(3):
            variant_list.append(
                shift_rows(branch_grad[:, :, branch + 1, :], (row_tap - 1) * dilation, fetch_grads)
            )
    variants = jnp.stack(variant_list, 2)
    stacked = make_kernel_taps(variants, dilation_rates).reshape(pixels, 28, own_width)
    input_grad = lax.psum_scatter(
        jnp.einsum("pto,tco->cp", stacked, all_weights, preferred_element_type=jnp.float32),
        "filt",
        scatter_dimension=0,
        tiled=True,
    ).T
    feature_grad = input_grad.astype(jnp.bfloat16).reshape(height, breadth, own_channels)
    return (head_output, feature_grad)


def solution(mesh):
    in_specs = (
        P("rows", None, None),
        P(None, "filt"),
        P(None, None, None, None, "filt"),
        P(None, "filt"),
        P(),
        P(),
        P("rows", None, None),
    )
    out_specs = (P("rows", None, "filt"), P("rows", None, "filt"))
    return jax.shard_map(
        on_device, mesh=mesh, in_specs=in_specs, out_specs=out_specs, check_vma=False
    )
```

profile of v0, /device:TPU:0, one launch (start us, length us, event | category | flops | bytes accessed | tf_op | source)
XLA Modules:
  0.0 257.3 jit_solution(13398070926808505381)
XLA Ops:
  7.2 1.6 copy-done
  8.8 9.5 %fusion.3 = f32[576,28,64]{0,2,1:T(8,128)} fusion(bf16[576,2048,1]{1,0,2:T(8,128)(2,1)S(1)} %bitcast.201, bf16[27,2048,64]{1,2,0:T(8,128)(2,1)} %bitcast.237, bf16[1,2048,64]{1,2,0:T(8,128)(2,1)} %bitcast.239), kind=kOutput, calls=%fused_computation.4 | convolution fusion | flops 4231528448 | bytes 13828096 | tf_op jit(solution)/shard_map/pc,tco->pto/dot_general | solution.py:77
  18.4 7.6 %copy.97 = f32[576,28,64]{2,0,1:T(8,128)} copy(f32[576,28,64]{0,2,1:T(8,128)} %fusion.3) | data formatting | bytes 8257536 | tf_op jit(solution)/shard_map/pc,tco->pto/dot_general | solution.py:77
  25.9 2.8 %slice_bitcast_fusion.23 = (f32[12,48,64]{2,1,0:T(8,128)S(1)}, f32[12,48,64]{2,1,0:T(8,128)S(1)}, f32[12,48,64]{2,1,0:T(8,128)S(1)}, f32[12,48,64]{2,1,0:T(8,128...) fusion(f32[12,48,28,64]{3,1,0,2:T(8,128)} %bitcast.202), kind=kLoop, calls=%fused_computation.63 | loop fusion | bytes 5308416 | tf_op jit(solution)/shard_map/squeeze | solution.py:88
  30.0 4.9 %collective-permute-start = (f32[12,48,64]{2,1,0:T(8,128)S(1)}, f32[12,48,64]{2,1,0:T(8,128)S(1)}, u32[]{:S(2)}, u32[]{:S(2)}) collective-permute-start(f32[12,48,64]{2,1,0:T(8,128)S(1)} %get-tuple-element.25), channel_id=1, source_target_pairs={{0,4},{4,8},{8,12},{12,16},{16,20},{20,24},{24,28},{1,5},{5,9},{9,... | collective-permute-start | bytes 442376 | tf_op jit(solution)/shard_map/ppermute | solution.py:14
  36.5 11.0 %collective-permute-done = f32[12,48,64]{2,1,0:T(8,128)S(1)} collective-permute-done((f32[12,48,64]{2,1,0:T(8,128)S(1)}, f32[12,48,64]{2,1,0:T(8,128)S(1)}, u32[]{:S(2)}, u32[]{:S(2)}) %collective-permute-start) | collective-permute-done | bytes 147488 | tf_op jit(solution)/shard_map/ppermute | solution.py:14
  47.5 1.6 fusion.33
  49.1 5.4 %collective-permute-start.2 = (f32[12,48,64]{2,1,0:T(8,128)S(1)}, f32[12,48,64]{2,1,0:T(8,128)S(1)}, u32[]{:S(2)}, u32[]{:S(2)}) collective-permute-start(f32[12,48,64]{2,1,0:T(8,128)S(1)} %get-tuple-element.6), channel_id=1, source_target_pairs={{0,8},{4,12},{8,16},{12,20},{16,24},{20,28},{1,9},{5,13},{9,17},{1... | collective-permute-start | bytes 442376 | tf_op jit(solution)/shard_map/ppermute | solution.py:14
  55.7 4.6 %collective-permute-start.4 = (f32[12,48,64]{2,1,0:T(8,128)S(1)}, f32[12,48,64]{2,1,0:T(8,128)S(1)}, u32[]{:S(2)}, u32[]{:S(2)}) collective-permute-start(f32[12,48,64]{2,1,0:T(8,128)S(1)} %get-tuple-element.4), channel_id=1, source_target_pairs={{0,12},{4,16},{8,20},{12,24},{16,28},{1,13},{5,17},{9,21},{13,25},... | collective-permute-start | bytes 442376 | tf_op jit(solution)/shard_map/ppermute | solution.py:14
  62.6 2.3 collective-permute-done.3
  65.0 2.4 collective-permute-done.4
  67.4 4.6 %collective-permute-done.5 = f32[12,48,64]{2,1,0:T(8,128)S(1)} collective-permute-done((f32[12,48,64]{2,1,0:T(8,128)S(1)}, f32[12,48,64]{2,1,0:T(8,128)S(1)}, u32[]{:S(2)}, u32[]{:S(2)}) %collective-permute-start.5) | collective-permute-done | bytes 147488 | tf_op jit(solution)/shard_map/ppermute | solution.py:14
  75.7 1.9 copy.100
  77.6 21.3 %all-gather.2.cloned.1.call-done = bf16[576,1024]{1,0:T(8,128)(2,1)} async-done(((bf16[576,256]{1,0:T(8,128)(2,1)}), bf16[576,1024]{1,0:T(8,128)(2,1)}) %all-gather.2.cloned.1.call-update) | async-done | bytes 1179664 | tf_op jit(solution)/shard_map/all_gather | solution.py:104
  98.9 2.7 %fusion.5 = (bf16[576,256]{1,0:T(8,128)(2,1)S(1)}, bf16[576,256]{1,0:T(8,128)(2,1)}) fusion(bf16[12,48,256]{2,1,0:T(8,128)(2,1)} %param.13, f32[256]{0:T(256)S(1)} %copy-done.23, bf16[576,1024]{1,0:T(8,128)(2,1)} %all-gather.2.cloned.1.call-done, bf16[1024,256]{1,0:T(8,128)(2,1)} %bitcast.234), kind=kOutput, calls=%fused_computation.11 | convolution fusion | flops 302874624 | bytes 2589696 | tf_op jit(solution)/shard_map/dot_general | solution.py:103
  105.6 4.5 %collective-permute-start.7 = (bf16[12,48,64]{2,1,0:T(8,128)(2,1)S(1)}, bf16[12,48,64]{2,1,0:T(8,128)(2,1)S(1)}, u32[]{:S(2)}, u32[]{:S(2)}) collective-permute-start(bf16[12,48,64]{2,1,0:T(8,128)(2,1)S(1)} %get-tuple-element.30), channel_id=1, source_target_pairs={{0,4},{4,8},{8,12},{12,16},{16,20},{20,24},{24,28},{1,5},{5,9},{9,... | collective-permute-start | bytes 221192 | tf_op jit(solution)/shard_map/ppermute | solution.py:14
  112.2 5.2 %collective-permute-start.9 = (bf16[12,48,64]{2,1,0:T(8,128)(2,1)S(1)}, bf16[12,48,64]{2,1,0:T(8,128)(2,1)}, u32[]{:S(2)}, u32[]{:S(2)}) collective-permute-start(bf16[12,48,64]{2,1,0:T(8,128)(2,1)S(1)} %get-tuple-element.31), channel_id=1, source_target_pairs={{0,8},{4,12},{8,16},{12,20},{16,24},{20,28},{1,9},{5,13},{9,17},{1... | collective-permute-start | bytes 221192 | tf_op jit(solution)/shard_map/ppermute | solution.py:14
  132.6 5.6 %collective-permute-start.11 = (bf16[12,48,64]{2,1,0:T(8,128)(2,1)}, bf16[12,48,64]{2,1,0:T(8,128)(2,1)S(1)}, u32[]{:S(2)}, u32[]{:S(2)}) collective-permute-start(bf16[12,48,64]{2,1,0:T(8,128)(2,1)} %get-tuple-element.32), channel_id=1, source_target_pairs={{0,12},{4,16},{8,20},{12,24},{16,28},{1,13},{5,17},{9,21},{13,25},... | collective-permute-start | bytes 221192 | tf_op jit(solution)/shard_map/ppermute | solution.py:14
  138.4 1.6 fusion.48
  140.0 1.6 fusion.46
  149.4 1.7 copy.112
  156.3 1.7 copy.121
  161.1 1.6 constant_dynamic-update-slice_fusion.26
  164.2 1.5 constant_dynamic-update-slice_fusion.24
  167.7 1.5 constant_dynamic-update-slice_fusion.20
  170.7 1.5 constant_dynamic-update-slice_fusion.18
  172.2 1.5 constant_dynamic-update-slice_fusion.17
  178.7 1.5 constant_dynamic-update-slice_fusion.11
  183.9 1.5 constant_dynamic-update-slice_fusion.7
  189.9 10.3 %fusion.2 = f32[2048,576]{0,1:T(8,128)} fusion(bf16[576,28,64]{0,2,1:T(8,128)(2,1)} %constant_dynamic-update-slice_fusion, bf16[27,2048,64]{1,2,0:T(8,128)(2,1)} %bitcast.238, bf16[1,2048,64]{1,2,0:T(8,128)(2,1)S(1)} %bitcast.240), kind=kOutput, calls=%fused_computation.3 | convolution fusion | flops 4231528448 | bytes 14123008 | tf_op jit(solution)/shard_map/pto,tco->cp/dot_general | solution.py:127
  202.0 46.2 %reduce-scatter.2.cloned.1.call-done = f32[512,576]{0,1:T(8,128)} async-done(((f32[2048,576]{0,1:T(8,128)}), f32[512,576]{0,1:T(8,128)}) %reduce-scatter.2.cloned.1.call-update) | async-done | bytes 1179664 | tf_op jit(solution)/shard_map/reduce_scatter | solution.py:126
  248.3 2.2 convert_element_type.83
  (165 shorter events, 67.1 us)
Async XLA Ops:
  7.2 91.7 %all-gather.2.cloned.1.call-start = ((), (), s32[]{:S(2)}) async-start(), calls=%async_computation.1 | async-start | bytes 1474560 | tf_op jit(solution)/shard_map/all_gather | solution.py:104
  30.0 17.4 %collective-permute-start = (f32[12,48,64]{2,1,0:T(8,128)S(1)}, f32[12,48,64]{2,1,0:T(8,128)S(1)}, u32[]{:S(2)}, u32[]{:S(2)}) collective-permute-start(f32[12,48,64]{2,1,0:T(8,128)S(1)} %get-tuple-element.25), channel_id=1, source_target_pairs={{0,4},{4,8},{8,12},{12,16},{16,20},{20,24},{24,28},{1,5},{5,9},{9,... | collective-permute-start | bytes 442376 | tf_op jit(solution)/shard_map/ppermute | solution.py:14
  34.9 12.6 %collective-permute-start.1 = (f32[12,48,64]{2,1,0:T(8,128)S(1)}, f32[12,48,64]{2,1,0:T(8,128)S(1)}, u32[]{:S(2)}, u32[]{:S(2)}) collective-permute-start(f32[12,48,64]{2,1,0:T(8,128)S(1)} %get-tuple-element.26), channel_id=1, source_target_pairs={{4,0},{8,4},{12,8},{16,12},{20,16},{24,20},{28,24},{5,1},{9,5},{13... | collective-permute-start | bytes 442376 | tf_op jit(solution)/shard_map/ppermute | solution.py:14
  49.0 24.2 %copy-start.3 = (f32[12,48,1,64]{3,1,2,0:T(8,128)}, f32[12,48,1,64]{3,1,2,0:T(8,128)S(1)}, u32[]{:S(2)}) copy-start(f32[12,48,1,64]{3,1,2,0:T(8,128)S(1)} %get-tuple-element.2) | copy-start | bytes 442372
  49.1 13.6 %collective-permute-start.2 = (f32[12,48,64]{2,1,0:T(8,128)S(1)}, f32[12,48,64]{2,1,0:T(8,128)S(1)}, u32[]{:S(2)}, u32[]{:S(2)}) collective-permute-start(f32[12,48,64]{2,1,0:T(8,128)S(1)} %get-tuple-element.6), channel_id=1, source_target_pairs={{0,8},{4,12},{8,16},{12,20},{16,24},{20,28},{1,9},{5,13},{9,17},{1... | collective-permute-start | bytes 442376 | tf_op jit(solution)/shard_map/ppermute | solution.py:14
  54.4 10.5 %collective-permute-start.3 = (f32[12,48,64]{2,1,0:T(8,128)S(1)}, f32[12,48,64]{2,1,0:T(8,128)S(1)}, u32[]{:S(2)}, u32[]{:S(2)}) collective-permute-start(f32[12,48,64]{2,1,0:T(8,128)S(1)} %get-tuple-element.5), channel_id=1, source_target_pairs={{8,0},{12,4},{16,8},{20,12},{24,16},{28,20},{9,1},{13,5},{17,9},{2... | collective-permute-start | bytes 442376 | tf_op jit(solution)/shard_map/ppermute | solution.py:14
  55.7 11.7 %collective-permute-start.4 = (f32[12,48,64]{2,1,0:T(8,128)S(1)}, f32[12,48,64]{2,1,0:T(8,128)S(1)}, u32[]{:S(2)}, u32[]{:S(2)}) collective-permute-start(f32[12,48,64]{2,1,0:T(8,128)S(1)} %get-tuple-element.4), channel_id=1, source_target_pairs={{0,12},{4,16},{8,20},{12,24},{16,28},{1,13},{5,17},{9,21},{13,25},... | collective-permute-start | bytes 442376 | tf_op jit(solution)/shard_map/ppermute | solution.py:14
  60.4 11.7 %collective-permute-start.5 = (f32[12,48,64]{2,1,0:T(8,128)S(1)}, f32[12,48,64]{2,1,0:T(8,128)S(1)}, u32[]{:S(2)}, u32[]{:S(2)}) collective-permute-start(f32[12,48,64]{2,1,0:T(8,128)S(1)} %get-tuple-element.3), channel_id=1, source_target_pairs={{12,0},{16,4},{20,8},{24,12},{28,16},{13,1},{17,5},{21,9},{25,13},... | collective-permute-start | bytes 442376 | tf_op jit(solution)/shard_map/ppermute | solution.py:14
  74.0 24.9 %copy-start.23 = (f32[256]{0:T(256)S(1)}, f32[256]{0:T(256)}, u32[]{:S(2)}) copy-start(f32[256]{0:T(256)} %param.12) | copy-start | bytes 3076
  75.6 26.0 %copy-start.2 = (f32[12,48,1,64]{3,1,2,0:T(8,128)S(1)}, f32[12,48,1,64]{3,1,2,0:T(8,128)}, u32[]{:S(2)}) copy-start(f32[12,48,1,64]{3,1,2,0:T(8,128)} %copy-done.1) | copy-start | bytes 442372
  75.6 26.0 %copy-start.4 = (f32[12,48,1,64]{3,1,2,0:T(8,128)S(1)}, f32[12,48,1,64]{3,1,2,0:T(8,128)}, u32[]{:S(2)}) copy-start(f32[12,48,1,64]{3,1,2,0:T(8,128)} %copy-done.3) | copy-start | bytes 442372
  75.6 172.7 %reduce-scatter.2.cloned.1.call-start = ((), (), s32[]{:S(2)}) async-start(), calls=%async_computation.2 | async-start | bytes 5898240 | tf_op jit(solution)/shard_map/reduce_scatter | solution.py:126
  103.6 29.0 %collective-permute-start.6 = (bf16[12,48,64]{2,1,0:T(8,128)(2,1)S(1)}, bf16[12,48,64]{2,1,0:T(8,128)(2,1)S(1)}, u32[]{:S(2)}, u32[]{:S(2)}) collective-permute-start(bf16[12,48,64]{2,1,0:T(8,128)(2,1)S(1)} %get-tuple-element.30), channel_id=1, source_target_pairs={{4,0},{8,4},{12,8},{16,12},{20,16},{24,20},{28,24},{5,1},{9,5},{13... | collective-permute-start | bytes 221192 | tf_op jit(solution)/shard_map/ppermute | solution.py:14
  105.6 32.7 %collective-permute-start.7 = (bf16[12,48,64]{2,1,0:T(8,128)(2,1)S(1)}, bf16[12,48,64]{2,1,0:T(8,128)(2,1)S(1)}, u32[]{:S(2)}, u32[]{:S(2)}) collective-permute-start(bf16[12,48,64]{2,1,0:T(8,128)(2,1)S(1)} %get-tuple-element.30), channel_id=1, source_target_pairs={{0,4},{4,8},{8,12},{12,16},{16,20},{20,24},{24,28},{1,5},{5,9},{9,... | collective-permute-start | bytes 221192 | tf_op jit(solution)/shard_map/ppermute | solution.py:14
  110.2 28.2 %collective-permute-start.8 = (bf16[12,48,64]{2,1,0:T(8,128)(2,1)S(1)}, bf16[12,48,64]{2,1,0:T(8,128)(2,1)}, u32[]{:S(2)}, u32[]{:S(2)}) collective-permute-start(bf16[12,48,64]{2,1,0:T(8,128)(2,1)S(1)} %get-tuple-element.31), channel_id=1, source_target_pairs={{8,0},{12,4},{16,8},{20,12},{24,16},{28,20},{9,1},{13,5},{17,9},{2... | collective-permute-start | bytes 221192 | tf_op jit(solution)/shard_map/ppermute | solution.py:14
  112.2 27.8 %collective-permute-start.9 = (bf16[12,48,64]{2,1,0:T(8,128)(2,1)S(1)}, bf16[12,48,64]{2,1,0:T(8,128)(2,1)}, u32[]{:S(2)}, u32[]{:S(2)}) collective-permute-start(bf16[12,48,64]{2,1,0:T(8,128)(2,1)S(1)} %get-tuple-element.31), channel_id=1, source_target_pairs={{0,8},{4,12},{8,16},{12,20},{16,24},{20,28},{1,9},{5,13},{9,17},{1... | collective-permute-start | bytes 221192 | tf_op jit(solution)/shard_map/ppermute | solution.py:14
  117.4 24.2 %collective-permute-start.10 = (bf16[12,48,64]{2,1,0:T(8,128)(2,1)}, bf16[12,48,64]{2,1,0:T(8,128)(2,1)}, u32[]{:S(2)}, u32[]{:S(2)}) collective-permute-start(bf16[12,48,64]{2,1,0:T(8,128)(2,1)} %get-tuple-element.32), channel_id=1, source_target_pairs={{12,0},{16,4},{20,8},{24,12},{28,16},{13,1},{17,5},{21,9},{25,13},... | collective-permute-start | bytes 221192 | tf_op jit(solution)/shard_map/ppermute | solution.py:14
  132.6 26.1 %collective-permute-start.11 = (bf16[12,48,64]{2,1,0:T(8,128)(2,1)}, bf16[12,48,64]{2,1,0:T(8,128)(2,1)S(1)}, u32[]{:S(2)}, u32[]{:S(2)}) collective-permute-start(bf16[12,48,64]{2,1,0:T(8,128)(2,1)} %get-tuple-element.32), channel_id=1, source_target_pairs={{0,12},{4,16},{8,20},{12,24},{16,28},{1,13},{5,17},{9,21},{13,25},... | collective-permute-start | bytes 221192 | tf_op jit(solution)/shard_map/ppermute | solution.py:14
  143.8 10.8 %copy-start.16 = (bf16[12,24,64]{2,1,0:T(8,128)(2,1)S(1)}, bf16[12,24,64]{2,1,0:T(8,128)(2,1)}, u32[]{:S(2)}) copy-start(bf16[12,24,64]{2,1,0:T(8,128)(2,1)} %get-tuple-element.42) | copy-start | bytes 110596
  146.2 9.3 %copy-start.18 = (bf16[12,12,64]{2,1,0:T(8,128)(2,1)S(1)}, bf16[12,12,64]{2,1,0:T(8,128)(2,1)}, u32[]{:S(2)}) copy-start(bf16[12,12,64]{2,1,0:T(8,128)(2,1)} %get-tuple-element.41) | copy-start | bytes 55300
  149.4 16.3 %copy-start.10 = (bf16[576,1,64]{0,2,1:T(8,128)(2,1)S(1)}, bf16[576,1,64]{0,2,1:T(8,128)(2,1)}, u32[]{:S(2)}) copy-start(bf16[576,1,64]{0,2,1:T(8,128)(2,1)} %copy.105) | copy-start | bytes 221188
  151.1 15.2 %copy-start.9 = (bf16[576,1,64]{0,2,1:T(8,128)(2,1)S(1)}, bf16[576,1,64]{0,2,1:T(8,128)(2,1)}, u32[]{:S(2)}) copy-start(bf16[576,1,64]{0,2,1:T(8,128)(2,1)} %copy.106) | copy-start | bytes 221188
  151.2 15.9 %copy-start.11 = (bf16[576,1,64]{0,2,1:T(8,128)(2,1)S(1)}, bf16[576,1,64]{0,2,1:T(8,128)(2,1)}, u32[]{:S(2)}) copy-start(bf16[576,1,64]{0,2,1:T(8,128)(2,1)} %copy.107) | copy-start | bytes 221188
  154.7 22.1 %copy-start.7 = (bf16[576,1,64]{0,2,1:T(8,128)(2,1)S(1)}, bf16[576,1,64]{0,2,1:T(8,128)(2,1)}, u32[]{:S(2)}) copy-start(bf16[576,1,64]{0,2,1:T(8,128)(2,1)} %copy.114) | copy-start | bytes 221188
  155.5 22.0 %copy-start.6 = (bf16[576,1,64]{0,2,1:T(8,128)(2,1)S(1)}, bf16[576,1,64]{0,2,1:T(8,128)(2,1)}, u32[]{:S(2)}) copy-start(bf16[576,1,64]{0,2,1:T(8,128)(2,1)} %copy.115) | copy-start | bytes 221188
  155.5 22.6 %copy-start.8 = (bf16[576,1,64]{0,2,1:T(8,128)(2,1)S(1)}, bf16[576,1,64]{0,2,1:T(8,128)(2,1)}, u32[]{:S(2)}) copy-start(bf16[576,1,64]{0,2,1:T(8,128)(2,1)} %copy.116) | copy-start | bytes 221188
  158.8 28.6 %copy-start.5 = (bf16[576,1,64]{0,2,1:T(8,128)(2,1)S(1)}, bf16[576,1,64]{0,2,1:T(8,128)(2,1)}, u32[]{:S(2)}) copy-start(bf16[576,1,64]{0,2,1:T(8,128)(2,1)} %copy.125) | copy-start | bytes 221188
  160.3 27.7 %copy-start.13 = (bf16[576,1,64]{0,2,1:T(8,128)(2,1)S(1)}, bf16[576,1,64]{0,2,1:T(8,128)(2,1)}, u32[]{:S(2)}) copy-start(bf16[576,1,64]{0,2,1:T(8,128)(2,1)} %copy.126) | copy-start | bytes 221188
  160.3 28.3 %copy-start.12 = (bf16[576,1,64]{0,2,1:T(8,128)(2,1)S(1)}, bf16[576,1,64]{0,2,1:T(8,128)(2,1)}, u32[]{:S(2)}) copy-start(bf16[576,1,64]{0,2,1:T(8,128)(2,1)} %copy.127) | copy-start | bytes 221188
  161.1 24.4 %copy-start.14 = (bf16[576,1,64]{0,2,1:T(8,128)(2,1)S(1)}, bf16[576,1,64]{0,2,1:T(8,128)(2,1)}, u32[]{:S(2)}) copy-start(bf16[576,1,64]{0,2,1:T(8,128)(2,1)} %copy.122) | copy-start | bytes 221188
  161.1 28.2 %copy-start.15 = (bf16[576,1,64]{0,2,1:T(8,128)(2,1)S(1)}, bf16[576,1,64]{0,2,1:T(8,128)(2,1)}, u32[]{:S(2)}) copy-start(bf16[576,1,64]{0,2,1:T(8,128)(2,1)} %copy.128) | copy-start | bytes 221188
  161.1 28.8 %copy-start.22 = (bf16[2048,64]{0,1:T(8,128)(2,1)S(1)}, bf16[2048,64]{0,1:T(8,128)(2,1)}, u32[]{:S(2)}) copy-start(bf16[2048,64]{0,1:T(8,128)(2,1)} %param.8) | copy-start | bytes 786436
  (6 other events, 24.8 us)
Sparse Core Ops, SparseCore 0:
  75.7 23.1 all-gather.1
  200.4 47.7 reduce-scatter.1
where the time goes:
time: 259 us; the launch traced here: 257 us
  waiting for transfers between devices  88 us (34%)
  local copies, waits for them, and re-layouts  84.9 us (33%)
  starting transfers between devices  38 us (15%)
  matrix products  23.8 us (9%)
  between operations  14.6 us (6%)
  other arithmetic  8.03 us (3%)
    reduce_scatter x1, waiting for transfers between devices, on_device(): lax.psum_scatter(jnp.einsum('pto,tco->cp', stacked, all_weights, preferre...  46.2 us
    ppermute x12, starting transfers between devices, passed_along(): return lax.ppermute(x, axis, pairs)  37.9 us
    unnamed x75, local copies, waits for them, and re-layouts  33 us
    another operation x29, local copies, waits for them, and re-layouts, make_kernel_taps(): return jnp.stack(stacked, 2)  22.8 us
    all_gather x1, waiting for transfers between devices, on_device(): lax.all_gather(activations, 'filt', axis=1, tiled=True)  21.3 us
    ppermute x12, waiting for transfers between devices, passed_along(): return lax.ppermute(x, axis, pairs)  20.4 us
    dot_general x1, matrix products, on_device(): jnp.einsum('pto,tco->cp', stacked, all_weights, preferred_element_type=jn...  10.3 us
    dot_general x1, matrix products, on_device(): jnp.einsum('pc,tco->pto', flattened, all_weights, preferred_element_type=...  9.52 us
  transfers between devices with their start and end apart: 14, of which 6 were waited for; matrix products, arithmetic and copies ran while one was open for 15% of the time, Pallas kernels for 0%

commit v1 on v0

--- a/solution.py
+++ b/solution.py
@@ -1,6 +1,11 @@
+import functools
+
 import jax
 import jax.numpy as jnp
+import numpy as np
 from jax import lax
+from jax.experimental import pallas as pl
+from jax.experimental.pallas import tpu as pltpu
 from jax.sharding import PartitionSpec as P
 
 FIRST_DILATION = 12
@@ -58,7 +63,7 @@
     return jnp.stack(stacked, 2)
 
 
-def on_device(
+def on_device_general(
     features, point_weight, dilated_weight, branch_bias, project_weight, project_bias, cotangent
 ):
     height, breadth, channels = features.shape
@@ -133,7 +138,439 @@
     return (head_output, feature_grad)
 
 
+W = 64
+BLOCK = 144
+PIXELS = 576
+HALF = 288
+CHANNELS = 2048
+F32 = jnp.float32
+BF16 = jnp.bfloat16
+VMEM_BYTES = 60 * 2**20
+
+OUT_PAIRS = ((3, 1), (1, 1), (2, 1), (3, 0), (1, 0), (2, 0), (1, 2), (2, 2), (3, 2))
+OUT_TAPS = [(k, i, j) for k, j in OUT_PAIRS for i in (0, 2)]
+OWN_TAPS = [(k, 1, j) for j in (1, 0, 2) for k in (1, 2, 3)]
+GRAD_TAPS = (
+    [(k, 1, 1) for k in (1, 2, 3)]
+    + OUT_TAPS
+    + [(k, 1, j) for k in (1, 2, 3) for j in (0, 2)]
+)
+
+
+def fits(mesh):
+    return mesh.shape["rows"] == 8 and mesh.shape["filt"] == 4
+
+
+def order_matrix():
+    to = np.zeros((192, 192), np.float32)
+    for m in range(4):
+        for r in range(4):
+            for c in range(12):
+                to[m * 48 + r * 12 + c, r * 48 + m * 12 + c] = 1
+    return to
+
+
+def tap_index(tap):
+    k, i, j = tap
+    return (k - 1) * 9 + i * 3 + j
+
+
+def nt(a, b):
+    return lax.dot_general(a, b, (((1,), (1,)), ((), ())), preferred_element_type=F32)
+
+
+def nn(a, b):
+    return lax.dot_general(a, b, (((1,), (0,)), ((), ())), preferred_element_type=F32)
+
+
+def into_blocks(order, read, write):
+    for g in range(3):
+        moved = nn(order, read(g * 192)).astype(BF16)
+        for m in range(4):
+            write(m * BLOCK + g * 48, moved[m * 48 : (m + 1) * 48])
+
+
+def from_blocks(order_t, value, write):
+    for g in range(3):
+        parts = [value[m * BLOCK + g * 48 : m * BLOCK + g * 48 + 48] for m in range(4)]
+        write(g * 192, nn(order_t, jnp.concatenate(parts, 0)).astype(BF16))
+
+
+def low_lanes(shape):
+    return lax.broadcasted_iota(jnp.int32, shape, 1) % 128 < W
+
+
+def outward_kernel(features, dilated, order, *refs):
+    plus, minus = refs[0:3], refs[3:6]
+    ordered, raw, weights, sums, feature_sems, weight_sems = refs[6:]
+    loads = []
+    for g in range(3):
+        rows = pl.ds(g * 192, 192)
+        loads.append(pltpu.make_async_copy(features.at[rows], raw.at[rows], feature_sems.at[g]))
+        loads[-1].start()
+    fetches = []
+    for q, tap in enumerate(OUT_TAPS):
+        fetches.append(
+            pltpu.make_async_copy(
+                dilated.at[tap_index(tap)], weights.at[pl.ds(q * W, W)], weight_sems.at[q]
+            )
+        )
+        fetches[-1].start()
+
+    for g in range(3):
+        loads[g].wait()
+        moved = nn(order[...], raw[g * 192 : (g + 1) * 192, :]).astype(BF16)
+        for m in range(4):
+            at = m * BLOCK + g * 48
+            ordered[at : at + 48, :] = moved[m * 48 : (m + 1) * 48]
+
+    def product(pair, pairs, first, last):
+        for q in range(2 * pair, 2 * (pair + pairs)):
+            fetches[q].wait()
+        return nt(
+            ordered[first * BLOCK : last * BLOCK, :],
+            weights[pair * 128 : (pair + pairs) * 128, :],
+        )
+
+    def add(k, first, value):
+        rows = slice(first * BLOCK, first * BLOCK + value.shape[0])
+        sums[k - 1, rows, :] = sums[k - 1, rows, :] + value
+
+    d = product(0, 2, 0, 4)
+    sums[2] = d[:, :128]
+    sums[0] = d[:, 128:]
+    d = product(2, 2, 0, 4)
+    sums[1] = d[:, :128]
+    add(3, 3, d[:BLOCK, 128:])
+    d = product(4, 2, 0, 3)
+    add(1, 1, d[:, :128])
+    add(2, 2, d[: 2 * BLOCK, 128:])
+    d = product(6, 2, 1, 4)
+    add(1, 0, d[:, :128])
+    add(2, 0, d[BLOCK:, 128:])
+    d = product(8, 1, 3, 4)
+    add(3, 0, d)
+
+    low = low_lanes((HALF, 128))
+    for k in range(3):
+        top, bottom = sums[k, :HALF, :], sums[k, HALF:, :]
+        plus[k][...] = jnp.where(low, top, pltpu.roll(bottom, W, 1))
+        minus[k][...] = jnp.where(low, pltpu.roll(top, W, 1), bottom)
+
+
+def outward_sums(features, dilated, order):
+    flops = 2 * PIXELS * CHANNELS * 18 * W
+    sent = jax.ShapeDtypeStruct((HALF, 128), F32)
+    return pl.pallas_call(
+        outward_kernel,
+        out_shape=[sent] * 6 + [jax.ShapeDtypeStruct((PIXELS, CHANNELS), BF16)],
+        in_specs=[
+            pl.BlockSpec(memory_space=pl.ANY),
+            pl.BlockSpec(memory_space=pl.ANY),
+            pl.BlockSpec(memory_space=pltpu.VMEM),
+        ],
+        out_specs=[pl.BlockSpec(memory_space=pltpu.VMEM)] * 7,
+        scratch_shapes=[
+            pltpu.VMEM((PIXELS, CHANNELS), BF16),
+            pltpu.VMEM((18 * W, CHANNELS), BF16),
+            pltpu.VMEM((3, PIXELS, 128), F32),
+            pltpu.SemaphoreType.DMA((3,)),
+            pltpu.SemaphoreType.DMA((18,)),
+        ],
+        compiler_params=pltpu.CompilerParams(vmem_limit_bytes=VMEM_BYTES),
+        cost_estimate=pl.CostEstimate(flops=flops, bytes_accessed=9 * 10**6, transcendentals=0),
+        name="outward_sums",
+    )(features, dilated, order)
+
+
+def own_kernel(ordered, dilated, point, bias, out, weights, sems):
+    fetches = [pltpu.make_async_copy(point, weights.at[pl.ds(0, W)], sems.at[9])]
+    for q, tap in enumerate(OWN_TAPS):
+        fetches.append(
+            pltpu.make_async_copy(
+                dilated.at[tap_index(tap)], weights.at[pl.ds((q + 1) * W, W)], sems.at[q]
+            )
+        )
+    for fetch in fetches:
+        fetch.start()
+    for fetch in fetches[:4]:
+        fetch.wait()
+    out[...] = nt(ordered[...], weights[:256, :]) + bias[...]
+    low = low_lanes((PIXELS, 128))
+
+    def add(first, value, k):
+        lanes = slice(0, 128) if k == 1 else slice(128, 256)
+        rows = slice(first * BLOCK, first * BLOCK + value.shape[0])
+        mask = low[: value.shape[0]]
+        kept = jnp.where(mask, value[:, lanes], 0.0) if k == 2 else jnp.where(mask, 0.0, value[:, lanes])
+        out[rows, lanes] = out[rows, lanes] + kept
+
+    for fetch in fetches[4:7]:
+        fetch.wait()
+    d = nt(ordered[: 3 * BLOCK, :], weights[192:448, :])
+    for k in (1, 2, 3):
+        add(k, d[: (4 - k) * BLOCK], k)
+    for fetch in fetches[7:]:
+        fetch.wait()
+    d = nt(ordered[BLOCK:, :], weights[384:640, :])
+    for k in (1, 2, 3):
+        add(0, d[(k - 1) * BLOCK :], k)
+
+
+def own_sums(ordered, dilated, point, bias):
+    flops = 2 * PIXELS * CHANNELS * 10 * W
+    return pl.pallas_call(
+        own_kernel,
+        out_shape=jax.ShapeDtypeStruct((PIXELS, 4 * W), F32),
+        in_specs=[
+            pl.BlockSpec(memory_space=pltpu.VMEM),
+            pl.BlockSpec(memory_space=pl.ANY),
+            pl.BlockSpec(memory_space=pl.ANY),
+            pl.BlockSpec(memory_space=pltpu.VMEM),
+        ],
+        out_specs=pl.BlockSpec(memory_space=pltpu.VMEM),
+        scratch_shapes=[
+            pltpu.VMEM((10 * W, CHANNELS), BF16),
+            pltpu.SemaphoreType.DMA((10,)),
+        ],
+        compiler_params=pltpu.CompilerParams(vmem_limit_bytes=VMEM_BYTES),
+        cost_estimate=pl.CostEstimate(flops=flops, bytes_accessed=6 * 10**6, transcendentals=0),
+        name="own_sums",
+    )(ordered, dilated, point, bias)
+
+
+def activation_kernel(own, *refs):
+    recv, acts = refs[:6], refs[6]
+    low = low_lanes((HALF, 128))
+    t1, t2, t3 = (recv[k][...] + recv[k + 3][...] for k in range(3))
+    r1, r2, r3 = (pltpu.roll(t, W, 1) for t in (t1, t2, t3))
+    for rows, a, b, c in ((slice(0, HALF), r1, t2, r3), (slice(HALF, PIXELS), t1, r2, t3)):
+        left = own[rows, :128] + jnp.where(low, 0.0, a)
+        right = own[rows, 128:] + jnp.where(low, b, c)
+        acts[rows, :128] = jnp.maximum(left, 0.0).astype(BF16)
+        acts[rows, 128:] = jnp.maximum(right, 0.0).astype(BF16)
+
+
+def activations_of(own, received):
+    return pl.pallas_call(
+        activation_kernel,
+        out_shape=jax.ShapeDtypeStruct((PIXELS, 4 * W), BF16),
+        in_specs=[pl.BlockSpec(memory_space=pltpu.VMEM)] * 7,
+        out_specs=pl.BlockSpec(memory_space=pltpu.VMEM),
+        compiler_params=pltpu.CompilerParams(vmem_limit_bytes=VMEM_BYTES),
+        name="activations",
+    )(own, *received)
+
+
+def head_kernel(member_ref, a0, a1, a2, a3, project, bias, cotangent, order, order_t, *refs):
+    head_out, grads, sends, ordered = refs[0], refs[1], refs[2:5], refs[5]
+    member = member_ref[0]
+
+    def rows_of(who):
+        at = pl.multiple_of(who * W, W)
+        return jnp.concatenate([project[k, pl.ds(at, W), :] for k in range(4)], 0)
+
+    own_rows = rows_of(member)
+    pre = nn(a0[...], own_rows) + bias[...]
+    for flip, acts in ((1, a1), (2, a2), (3, a3)):
+        pre = pre + nn(acts[...], rows_of(member ^ flip))
+    mine = jnp.zeros((PIXELS, W), F32)
+    for q in range(4):
+        mine = mine + jnp.where(member == q, pre[:, q * W : (q + 1) * W], 0.0)
+    mine = jnp.maximum(mine, 0.0).astype(BF16)
+
+    def put(at, value):
+        head_out[at : at + 192, :] = value
+
+    from_blocks(order_t[...], mine, put)
+    for g in range(3):
+        moved = nn(order[...], cotangent[g * 192 : (g + 1) * 192, :])
+        for m in range(4):
+            at = m * BLOCK + g * 48
+            ordered[at : at + 48, :] = moved[m * 48 : (m + 1) * 48]
+    head_grad = jnp.where(pre > 0, ordered[...], 0.0).astype(BF16)
+    act_grad = nt(head_grad, own_rows)
+    grad = jnp.where(a0[...].astype(F32) > 0, act_grad, 0.0)
+    grads[...] = grad.astype(BF16)
+    low = low_lanes((HALF, 128))
+    left, right = grad[:, :128], grad[:, 128:]
+    sends[0][...] = jnp.where(low, pltpu.roll(left[:HALF], W, 1), left[HALF:]).astype(BF16)
+    sends[1][...] = jnp.where(low, right[:HALF], pltpu.roll(right[HALF:], W, 1)).astype(BF16)
+    sends[2][...] = jnp.where(low, pltpu.roll(right[:HALF], W, 1), right[HALF:]).astype(BF16)
+
+
+def head(member, acts, project, bias, cotangent, order, order_t):
+    sent = jax.ShapeDtypeStruct((HALF, 128), BF16)
+    return pl.pallas_call(
+        head_kernel,
+        out_shape=[
+            jax.ShapeDtypeStruct((PIXELS, W), BF16),
+            jax.ShapeDtypeStruct((PIXELS, 4 * W), BF16),
+            sent,
+            sent,
+            sent,
+        ],
+        in_specs=[pl.BlockSpec(memory_space=pltpu.SMEM)]
+        + [pl.BlockSpec(memory_space=pltpu.VMEM)] * 9,
+        out_specs=[pl.BlockSpec(memory_space=pltpu.VMEM)] * 5,
+        scratch_shapes=[pltpu.VMEM((PIXELS, 256), F32)],
+        compiler_params=pltpu.CompilerParams(vmem_limit_bytes=VMEM_BYTES),
+        name="head",
+    )(member, *acts, project, bias, cotangent, order, order_t)
+
+
+def grad_kernel(where_ref, own, *refs):
+    recv, dilated, point = refs[:6], refs[6], refs[7]
+    away, kept, stack, pairs, twice, weights, sems = refs[8:]
+    first = pl.multiple_of(where_ref[0], 1024)
+    columns = pl.ds(first, 1024)
+    fetches = [
+        pltpu.make_async_copy(point.at[:, columns], weights.at[pl.ds(0, W)], sems.at[27])
+    ]
+    for q, tap in enumerate(GRAD_TAPS):
+        fetches.append(
+            pltpu.make_async_copy(
+                dilated.at[tap_index(tap), :, columns],
+                weights.at[pl.ds((q + 1) * W, W)],
+                sems.at[q],
+            )
+        )
+    for fetch in fetches:
+        fetch.start()
+    low = low_lanes((HALF, 128))
+    for k in range(3):
+        p, m = recv[k][...].astype(F32), recv[k + 3][...].astype(F32)
+        pairs[k, :HALF, :] = jnp.where(low, p, pltpu.roll(m, W, 1)).astype(BF16)
+        pairs[k, HALF:, :] = jnp.where(low, pltpu.roll(p, W, 1), m).astype(BF16)
+        g = own[:, :128].astype(F32) if k == 0 else own[:, 128:].astype(F32)
+        other = pltpu.roll(g, W, 1)
+        low_all = low_lanes((PIXELS, 128))
+        both = jnp.where(low_all, g, other) if k == 1 else jnp.where(low_all, other, g)
+        twice[k] = both.astype(BF16)
+    stack[:, :256] = own[...]
+    nothing = jnp.zeros((BLOCK, 128), BF16)
+    for q, (k, j) in enumerate(OUT_PAIRS):
+        lanes = slice(256 + q * 128, 384 + q * 128)
+        for m in range(4):
+            source = m - (j - 1) * k
+            value = nothing
+            if 0 <= source < 4:
+                value = pairs[k - 1, source * BLOCK : (source + 1) * BLOCK, :]
+            stack[m * BLOCK : (m + 1) * BLOCK, lanes] = value
+    low_block = low_lanes((BLOCK, 128))
+    for k in (1, 2, 3):
+        lanes = slice(1408 + (k - 1) * 128, 1536 + (k - 1) * 128)
+        for m in range(4):
+            halves = []
+            for source in (m + k, m - k):
+                value = nothing
+                if 0 <= source < 4:
+                    value = twice[k - 1, source * BLOCK : (source + 1) * BLOCK, :]
+                halves.append(value)
+            stack[m * BLOCK : (m + 1) * BLOCK, lanes] = jnp.where(low_block, *halves)
+    for fetch in fetches:
+        fetch.wait()
+    core = where_ref[1]
+    for part, out in ((1 - core, away), (core, kept)):
+        for n in range(2):
+            at = pl.multiple_of(part * 512 + n * 256, 256)
+            out[:, n * 256 : (n + 1) * 256] = nn(stack[...], weights[:, pl.ds(at, 256)]).astype(BF16)
+
+
+def grad_half(where, own, received, dilated, point):
+    out = jax.ShapeDtypeStruct((PIXELS, 512), BF16)
+    return pl.pallas_call(
+        grad_kernel,
+        out_shape=[out, out],
+        in_specs=[pl.BlockSpec(memory_space=pltpu.SMEM)]
+        + [pl.BlockSpec(memory_space=pltpu.VMEM)] * 7
+        + [pl.BlockSpec(memory_space=pl.ANY)] * 2,
+        out_specs=[pl.BlockSpec(memory_space=pltpu.VMEM)] * 2,
+        scratch_shapes=[
+            pltpu.VMEM((PIXELS, 28 * W), BF16),
+            pltpu.VMEM((3, PIXELS, 128), BF16),
+            pltpu.VMEM((3, PIXELS, 128), BF16),
+            pltpu.VMEM((28 * W, 1024), BF16),
+            pltpu.SemaphoreType.DMA((28,)),
+        ],
+        compiler_params=pltpu.CompilerParams(vmem_limit_bytes=VMEM_BYTES),
+        cost_estimate=pl.CostEstimate(
+            flops=2 * PIXELS * 28 * W * 1024, bytes_accessed=6 * 10**6, transcendentals=0
+        ),
+        name="grad_half",
+    )(where, own, *received, dilated, point)
+
+
+def last_kernel(a, b, c, order_t, out):
+    total = a[...].astype(F32) + b[...].astype(F32) + c[...].astype(F32)
+
+    def put(at, value):
+        out[at : at + 192, :] = value
+
+    from_blocks(order_t[...], total.astype(BF16), put)
+
+
+def last_sum(a, b, c, order_t):
+    return pl.pallas_call(
+        last_kernel,
+        out_shape=jax.ShapeDtypeStruct((PIXELS, 512), BF16),
+        in_specs=[pl.BlockSpec(memory_space=pltpu.VMEM)] * 4,
+        out_specs=pl.BlockSpec(memory_space=pltpu.VMEM),
+        compiler_params=pltpu.CompilerParams(vmem_limit_bytes=VMEM_BYTES),
+        name="last_sum",
+    )(a, b, c, order_t)
+
+
+def flipped(x, bit):
+    return lax.ppermute(x, "filt", [(i, i ^ bit) for i in range(lax.axis_size("filt"))])
+
+
+def on_device(
+    features, point_weight, dilated_weight, branch_bias, project_weight, project_bias, cotangent
+):
+    member = lax.axis_index("filt")
+    order = jnp.asarray(order_matrix(), BF16)
+    order_t = jnp.asarray(order_matrix().T, BF16)
+    flat = features.reshape(PIXELS, CHANNELS)
+    dilated = jnp.transpose(dilated_weight, (0, 1, 2, 4, 3)).reshape(27, W, CHANNELS)
+    point = point_weight.T
+    bias = branch_bias.reshape(1, 4 * W)
+    *sums, ordered = outward_sums(flat, dilated, order)
+    received = [
+        passed_along(sums[3 * way + k], "rows", (1 - 2 * way) * (k + 1))
+        for way in range(2)
+        for k in range(3)
+    ]
+    own = own_sums(ordered, dilated, point, bias)
+    acts = activations_of(own, received)
+    across = flipped(acts, 2)
+    beside = flipped(acts, 1)
+    corner = flipped(across, 1)
+    head_output, grads, *sends = head(
+        member.astype(jnp.int32).reshape(1),
+        (acts, beside, across, corner),
+        project_weight,
+        project_bias.reshape(1, 256),
+        cotangent.reshape(PIXELS, 256),
+        order,
+        order_t,
+    )
+    arrived = [
+        passed_along(sends[k], "rows", (2 * way - 1) * (k + 1)) for way in range(2) for k in range(3)
+    ]
+    row, core = member // 2, member % 2
+    there = jnp.stack([(1 - row) * 1024, core]).astype(jnp.int32)
+    here = jnp.stack([row * 1024, core]).astype(jnp.int32)
+    away, kept = grad_half(there, grads, arrived, dilated, point)
+    crossing = (flipped(away, 1).astype(F32) + kept.astype(F32)).astype(BF16)
+    crossed = flipped(crossing, 2)
+    away, kept = grad_half(here, grads, arrived, dilated, point)
+    feature_grad = last_sum(kept, flipped(away, 1), crossed, order_t)
+    return head_output.reshape(12, 48, W), feature_grad.reshape(12, 48, 512)
+
+
 def solution(mesh):
+    body = on_device if fits(mesh) else on_device_general
     in_specs = (
         P("rows", None, None),
         P(None, "filt"),
@@ -145,5 +582,5 @@
     )
     out_specs = (P("rows", None, "filt"), P("rows", None, "filt"))
     return jax.shard_map(
-        on_device, mesh=mesh, in_specs=in_specs, out_specs=out_specs, check_vma=False
-    )
+        body, mesh=mesh, in_specs=in_specs, out_specs=out_specs, check_vma=False
+    )

time: 259 us -> 116 us (0.45)
  local copies, waits for them, and re-layouts: 84.9 us -> 3.48 us
  waiting for transfers between devices: 88 us -> 27 us
  Pallas kernels: 0 us -> 40.7 us
  matrix products: 23.8 us -> 0 us
  between operations: 14.6 us -> 0.98 us
  other arithmetic: 8.03 us -> 0.81 us
  starting transfers between devices: 38 us -> 42.8 us
    reduce_scatter x1 -> x0, waiting for transfers between devices: 46.2 us -> none  [on_device(): lax.psum_scatter(jnp.einsum('pto,tco->cp', stacked, all_weights, preferre...]
    pallas_call x0 -> x7, Pallas kernels: none -> 40.7 us  [the longest x2 13.7 us: grad_half(): pl.pallas_call(grad_kernel, out_shape=[out, out], in_specs=[pl.BlockSpec(...]
    unnamed x75 -> x38, local copies, waits for them, and re-layouts: 33 us -> 2.87 us
    dot_general x4 -> x0, matrix products: 23.8 us -> none  [the longest x1 10.3 us: on_device(): jnp.einsum('pto,tco->cp', stacked, all_weights, preferred_element_type=jn...]
    another operation x29 -> x0, local copies, waits for them, and re-layouts: 22.8 us -> none  [make_kernel_taps(): return jnp.stack(stacked, 2)]
    all_gather x1 -> x0, waiting for transfers between devices: 21.3 us -> none  [on_device(): lax.all_gather(activations, 'filt', axis=1, tiled=True)]
    ppermute x0 -> x6, waiting for transfers between devices: none -> 20.9 us  [flipped(): lax.ppermute(x, 'filt', [(i, i ^ bit) for i in range(lax.axis_size('filt'...]
    ppermute x12, waiting for transfers between devices: 20.4 us -> 6.1 us  [passed_along(): return lax.ppermute(x, axis, pairs)]
  transfers between devices with their start and end apart: 14 -> 18, of which waited for: 6 -> 8; matrix products, arithmetic and copies ran while one was open for 15% -> 1% of each run, Pallas kernels for 0% -> 12%
where the time goes in v1:
time: 116 us
  starting transfers between devices  42.8 us (37%)
  Pallas kernels  40.7 us (35%)
  waiting for transfers between devices  27 us (23%)
  local copies, waits for them, and re-layouts  3.48 us (3%)
    ppermute x12, starting transfers between devices, passed_along(): return lax.ppermute(x, axis, pairs)  39 us
    ppermute x6, waiting for transfers between devices, flipped(): lax.ppermute(x, 'filt', [(i, i ^ bit) for i in range(lax.axis_size('filt'...  20.9 us
    pallas_call x2, Pallas kernels, grad_half(): pl.pallas_call(grad_kernel, out_shape=[out, out], in_specs=[pl.BlockSpec(...  13.7 us
    pallas_call x1, Pallas kernels, outward_sums(): pl.pallas_call(outward_kernel, out_shape=[sent] * 6 + [jax.ShapeDtypeStru...  11.3 us
    pallas_call x1, Pallas kernels, own_sums(): pl.pallas_call(own_kernel, out_shape=jax.ShapeDtypeStruct((PIXELS, 4 * W)...  7.06 us
    ppermute x12, waiting for transfers between devices, passed_along(): return lax.ppermute(x, axis, pairs)  6.1 us
    ppermute x6, starting transfers between devices, flipped(): lax.ppermute(x, 'filt', [(i, i ^ bit) for i in range(lax.axis_size('filt'...  3.73 us
    pallas_call x1, Pallas kernels, head(): pl.pallas_call(head_kernel, out_shape=[jax.ShapeDtypeStruct((PIXELS, W),...  3.67 us
  transfers between devices with their start and end apart: 18, of which 8 were waited for; matrix products, arithmetic and copies ran while one was open for 1% of the time, Pallas kernels for 12%

profile of v1, /device:TPU:0, one launch (start us, length us, event | category | flops | bytes accessed | tf_op | source)
XLA Modules:
  0.0 115.7 jit_solution(9640852206333012009)
XLA Ops:
  0.6 11.3 %outward_sums.1 = (f32[288,128]{1,0:T(8,128)}, f32[288,128]{1,0:T(8,128)}, f32[288,128]{1,0:T(8,128)}, f32[288,128]{1,0:T(8,128)}, f32[288,128]{1,0:T(8,128)}, /...) custom-call(bf16[576,2048]{1,0:T(8,128)(2,1)} %bitcast.23, bf16[27,64,2048]{2,1,0:T(8,128)(2,1)} %bitcast.13, ...), custom_call_target="tpu_custom_call" | custom-call | flops 2717908992 | bytes 9000000 | tf_op jit(solution)/shard_map/outward_sums/pallas_call | solution.py:264
  12.0 4.9 %collective-permute-start = (f32[288,128]{1,0:T(8,128)}, f32[288,128]{1,0:T(8,128)S(1)}, u32[]{:S(2)}, u32[]{:S(2)}) collective-permute-start(f32[288,128]{1,0:T(8,128)} %get-tuple-element.19), channel_id=1, source_target_pairs={{0,4},{4,8},{8,12},{12,16},{16,20},{20,24},{24,28},{1,5},{5,9},{9,... | collective-permute-start | bytes 442376 | tf_op jit(solution)/shard_map/ppermute | solution.py:19
  16.9 3.5 %collective-permute-start.1 = (f32[288,128]{1,0:T(8,128)}, f32[288,128]{1,0:T(8,128)S(1)}, u32[]{:S(2)}, u32[]{:S(2)}) collective-permute-start(f32[288,128]{1,0:T(8,128)} %get-tuple-element.20), channel_id=1, source_target_pairs={{0,8},{4,12},{8,16},{12,20},{16,24},{20,28},{1,9},{5,13},{9,17},{1... | collective-permute-start | bytes 442376 | tf_op jit(solution)/shard_map/ppermute | solution.py:19
  20.3 4.5 %collective-permute-start.2 = (f32[288,128]{1,0:T(8,128)}, f32[288,128]{1,0:T(8,128)S(1)}, u32[]{:S(2)}, u32[]{:S(2)}) collective-permute-start(f32[288,128]{1,0:T(8,128)} %get-tuple-element.21), channel_id=1, source_target_pairs={{0,12},{4,16},{8,20},{12,24},{16,28},{1,13},{5,17},{9,21},{13,25},... | collective-permute-start | bytes 442376 | tf_op jit(solution)/shard_map/ppermute | solution.py:19
  24.8 1.3 %collective-permute-start.3 = (f32[288,128]{1,0:T(8,128)}, f32[288,128]{1,0:T(8,128)S(1)}, u32[]{:S(2)}, u32[]{:S(2)}) collective-permute-start(f32[288,128]{1,0:T(8,128)} %get-tuple-element.22), channel_id=1, source_target_pairs={{4,0},{8,4},{12,8},{16,12},{20,16},{24,20},{28,24},{5,1},{9,5},{13... | collective-permute-start | bytes 442376 | tf_op jit(solution)/shard_map/ppermute | solution.py:19
  26.1 1.3 %collective-permute-start.4 = (f32[288,128]{1,0:T(8,128)}, f32[288,128]{1,0:T(8,128)S(1)}, u32[]{:S(2)}, u32[]{:S(2)}) collective-permute-start(f32[288,128]{1,0:T(8,128)} %get-tuple-element.23), channel_id=1, source_target_pairs={{8,0},{12,4},{16,8},{20,12},{24,16},{28,20},{9,1},{13,5},{17,9},{2... | collective-permute-start | bytes 442376 | tf_op jit(solution)/shard_map/ppermute | solution.py:19
  27.4 1.3 %collective-permute-start.5 = (f32[288,128]{1,0:T(8,128)}, f32[288,128]{1,0:T(8,128)S(1)}, u32[]{:S(2)}, u32[]{:S(2)}) collective-permute-start(f32[288,128]{1,0:T(8,128)} %get-tuple-element.24), channel_id=1, source_target_pairs={{12,0},{16,4},{20,8},{24,12},{28,16},{13,1},{17,5},{21,9},{25,13},... | collective-permute-start | bytes 442376 | tf_op jit(solution)/shard_map/ppermute | solution.py:19
  28.7 0.6 reshape.31.bias
  29.4 7.1 %own_sums.1.own = f32[576,256]{1,0:T(8,128)} custom-call(bf16[576,2048]{1,0:T(8,128)(2,1)} %get-tuple-element.18.ordered, bf16[27,64,2048]{2,1,0:T(8,128)(2,1)} %bitcast.14, bf16[64,2048]{1,0:T(8,128)(2,1)} %bitcast.17, f32[1,256]{1,0:T(1,128)} %reshape.31.bias), custom_call_target="tpu_custom_call" | custom-call | flops 1509949440 | bytes 6000000 | tf_op jit(solution)/shard_map/own_sums/pallas_call | solution.py:322
  36.9 1.4 %collective-permute-done.5.refs_5_ = f32[288,128]{1,0:T(8,128)S(1)} collective-permute-done((f32[288,128]{1,0:T(8,128)}, f32[288,128]{1,0:T(8,128)S(1)}, u32[]{:S(2)}, u32[]{:S(2)}) %collective-permute-start.5) | collective-permute-done | bytes 147488 | tf_op jit(solution)/shard_map/ppermute | solution.py:19
  38.3 0.6 copy-done.17
  39.0 2.3 %activations.1.a0 = bf16[576,256]{1,0:T(8,128)(2,1)} custom-call(f32[576,256]{1,0:T(8,128)} %own_sums.1.own, f32[288,128]{1,0:T(8,128)} %copy-done.12, f32[288,128]{1,0:T(8,128)} %copy-done.13, f32[288,128]{1,0:T(8,128)} %copy-done.14, f32[288,128]{1,0:T(8,128)} %copy-done.15, f32[288,128]{1,0:T(8,128)} %copy-done.16, f32[288,128]{1,0:T(8,128)} %copy-done.17), custom_call_target="tpu_custom_call" | custom-call | tf_op jit(solution)/shard_map/activations/pallas_call | solution.py:355
  41.3 1.5 %collective-permute-start.7 = (bf16[576,256]{1,0:T(8,128)(2,1)}, bf16[576,256]{1,0:T(8,128)(2,1)S(1)}, u32[]{:S(2)}, u32[]{:S(2)}) collective-permute-start(bf16[576,256]{1,0:T(8,128)(2,1)} %activations.1.a0), channel_id=1, source_target_pairs={{0,2},{1,3},{2,0},{3,1},{4,6},{5,7},{6,4},{7,5},{8,10},{9,11},{10,... | collective-permute-start | bytes 884744 | tf_op jit(solution)/shard_map/ppermute | solution.py:525
  42.8 5.6 %collective-permute-done.7.a2 = bf16[576,256]{1,0:T(8,128)(2,1)S(1)} collective-permute-done((bf16[576,256]{1,0:T(8,128)(2,1)}, bf16[576,256]{1,0:T(8,128)(2,1)S(1)}, u32[]{:S(2)}, u32[]{:S(2)}) %collective-permute-start.7) | collective-permute-done | bytes 294944 | tf_op jit(solution)/shard_map/ppermute | solution.py:525
  48.4 1.6 %collective-permute-done.8.a3 = bf16[576,256]{1,0:T(8,128)(2,1)S(1)} collective-permute-done((bf16[576,256]{1,0:T(8,128)(2,1)S(1)}, bf16[576,256]{1,0:T(8,128)(2,1)S(1)}, u32[]{:S(2)}, u32[]{:S(2)}) %collective-permute-start.8) | collective-permute-done | bytes 294944 | tf_op jit(solution)/shard_map/ppermute | solution.py:525
  49.9 0.7 copy-done.5
  50.7 3.7 %head.1 = (bf16[576,64]{1,0:T(8,128)(2,1)}, bf16[576,256]{1,0:T(8,128)(2,1)}, bf16[288,128]{1,0:T(8,128)(2,1)}, bf16[288,128]{1,0:T(8,128)(2,1)}, bf16[288,128]{1,0:T(8,128)(2,1)}) custom-call(s32[1]{0:T(128)} %bitcast.member_ref, bf16[576,256]{1,0:T(8,128)(2,1)} %activations.1.a0, bf16[576,256]{1,0:T(8,128)(2,1)} %copy-done.4, bf16[576,256]{1,0:T(8,128)(2,1)} %copy-done.3, ...), custom_call_target="tpu_custom_call" | custom-call | tf_op jit(solution)/shard_map/head/pallas_call | solution.py:404
  54.4 1.3 %collective-permute-start.10 = (bf16[288,128]{1,0:T(8,128)(2,1)}, bf16[288,128]{1,0:T(8,128)(2,1)S(1)}, u32[]{:S(2)}, u32[]{:S(2)}) collective-permute-start(bf16[288,128]{1,0:T(8,128)(2,1)} %get-tuple-element.28), channel_id=1, source_target_pairs={{8,0},{12,4},{16,8},{20,12},{24,16},{28,20},{9,1},{13,5},{17,9},{2... | collective-permute-start | bytes 221192 | tf_op jit(solution)/shard_map/ppermute | solution.py:19
  55.7 6.4 %collective-permute-start.13 = (bf16[288,128]{1,0:T(8,128)(2,1)}, bf16[288,128]{1,0:T(8,128)(2,1)S(1)}, u32[]{:S(2)}, u32[]{:S(2)}) collective-permute-start(bf16[288,128]{1,0:T(8,128)(2,1)} %get-tuple-element.28), channel_id=1, source_target_pairs={{0,8},{4,12},{8,16},{12,20},{16,24},{20,28},{1,9},{5,13},{9,17},{1... | collective-permute-start | bytes 221192 | tf_op jit(solution)/shard_map/ppermute | solution.py:19
  62.1 1.3 %collective-permute-start.11 = (bf16[288,128]{1,0:T(8,128)(2,1)}, bf16[288,128]{1,0:T(8,128)(2,1)S(1)}, u32[]{:S(2)}, u32[]{:S(2)}) collective-permute-start(bf16[288,128]{1,0:T(8,128)(2,1)} %get-tuple-element.29), channel_id=1, source_target_pairs={{12,0},{16,4},{20,8},{24,12},{28,16},{13,1},{17,5},{21,9},{25,13},... | collective-permute-start | bytes 221192 | tf_op jit(solution)/shard_map/ppermute | solution.py:19
  63.4 5.8 %collective-permute-start.14 = (bf16[288,128]{1,0:T(8,128)(2,1)}, bf16[288,128]{1,0:T(8,128)(2,1)S(1)}, u32[]{:S(2)}, u32[]{:S(2)}) collective-permute-start(bf16[288,128]{1,0:T(8,128)(2,1)} %get-tuple-element.29), channel_id=1, source_target_pairs={{0,12},{4,16},{8,20},{12,24},{16,28},{1,13},{5,17},{9,21},{13,25},... | collective-permute-start | bytes 221192 | tf_op jit(solution)/shard_map/ppermute | solution.py:19
  69.2 6.1 %collective-permute-start.12 = (bf16[288,128]{1,0:T(8,128)(2,1)}, bf16[288,128]{1,0:T(8,128)(2,1)S(1)}, u32[]{:S(2)}, u32[]{:S(2)}) collective-permute-start(bf16[288,128]{1,0:T(8,128)(2,1)} %get-tuple-element.27), channel_id=1, source_target_pairs={{0,4},{4,8},{8,12},{12,16},{16,20},{20,24},{24,28},{1,5},{5,9},{9,... | collective-permute-start | bytes 221192 | tf_op jit(solution)/shard_map/ppermute | solution.py:19
  75.3 1.5 %collective-permute-start.9 = (bf16[288,128]{1,0:T(8,128)(2,1)}, bf16[288,128]{1,0:T(8,128)(2,1)S(1)}, u32[]{:S(2)}, u32[]{:S(2)}) collective-permute-start(bf16[288,128]{1,0:T(8,128)(2,1)} %get-tuple-element.27), channel_id=1, source_target_pairs={{4,0},{8,4},{12,8},{16,12},{20,16},{24,20},{28,24},{5,1},{9,5},{13... | collective-permute-start | bytes 221192 | tf_op jit(solution)/shard_map/ppermute | solution.py:19
  76.8 0.7 pad_add_fusion
  77.6 4.2 %collective-permute-done.9.refs_0_ = bf16[288,128]{1,0:T(8,128)(2,1)S(1)} collective-permute-done((bf16[288,128]{1,0:T(8,128)(2,1)}, bf16[288,128]{1,0:T(8,128)(2,1)S(1)}, u32[]{:S(2)}, u32[]{:S(2)}) %collective-permute-start.9) | collective-permute-done | bytes 73760 | tf_op jit(solution)/shard_map/ppermute | solution.py:19
  81.8 0.6 copy-done.11
  82.4 6.8 %grad_half.3 = (bf16[576,512]{1,0:T(8,128)(2,1)}, bf16[576,512]{1,0:T(8,128)(2,1)}) custom-call(s32[2]{0:T(128)} %get-tuple-element.35.where_ref, bf16[576,256]{1,0:T(8,128)(2,1)} %get-tuple-element.26.own, bf16[288,128]{1,0:T(8,128)(2,1)} %copy-done.11, bf16[288,128]{1,0:T(8,128)(2,1)} %copy-done.6, bf16[288,128]{1,0:T(8,128)(2,1)} %copy-done.8, ...), custom_call_target="tpu_custom_call" | custom-call | flops 2113929216 | bytes 6000000 | tf_op jit(solution)/shard_map/grad_half/pallas_call | solution.py:482
  89.3 6.9 %grad_half.2 = (bf16[576,512]{1,0:T(8,128)(2,1)}, bf16[576,512]{1,0:T(8,128)(2,1)}) custom-call(s32[2]{0:T(128)} %get-tuple-element.34.where_ref, bf16[576,256]{1,0:T(8,128)(2,1)} %get-tuple-element.26.own, bf16[288,128]{1,0:T(8,128)(2,1)} %copy-done.11, bf16[288,128]{1,0:T(8,128)(2,1)} %copy-done.6, bf16[288,128]{1,0:T(8,128)(2,1)} %copy-done.8, ...), custom_call_target="tpu_custom_call" | custom-call | flops 2113929216 | bytes 6000000 | tf_op jit(solution)/shard_map/grad_half/pallas_call | solution.py:482
  96.9 1.6 %collective-permute-start.17 = (bf16[576,512]{1,0:T(8,128)(2,1)S(1)}, bf16[576,512]{1,0:T(8,128)(2,1)S(1)}, u32[]{:S(2)}, u32[]{:S(2)}) collective-permute-start(bf16[576,512]{1,0:T(8,128)(2,1)S(1)} %add_convert_fusion), channel_id=1, source_target_pairs={{0,2},{1,3},{2,0},{3,1},{4,6},{5,7},{6,4},{7,5},{8,10},{9,11},{10,... | collective-permute-start | bytes 1769480 | tf_op jit(solution)/shard_map/ppermute | solution.py:525
  98.6 13.6 %collective-permute-done.17.c = bf16[576,512]{1,0:T(8,128)(2,1)S(1)} collective-permute-done((bf16[576,512]{1,0:T(8,128)(2,1)S(1)}, bf16[576,512]{1,0:T(8,128)(2,1)S(1)}, u32[]{:S(2)}, u32[]{:S(2)}) %collective-permute-start.17) | collective-permute-done | bytes 589856 | tf_op jit(solution)/shard_map/ppermute | solution.py:525
  112.2 0.8 copy-done.2
  113.1 2.7 %last_sum.1 = bf16[576,512]{1,0:T(8,128)(2,1)} custom-call(bf16[576,512]{1,0:T(8,128)(2,1)} %get-tuple-element.30.a, bf16[576,512]{1,0:T(8,128)(2,1)} %copy-done.1, bf16[576,512]{1,0:T(8,128)(2,1)} %copy-done.2, bf16[192,192]{1,0:T(8,128)(2,1)} %constant.33.clone.order.order_t), custom_call_target="tpu_custom_call" | custom-call | tf_op jit(solution)/shard_map/last_sum/pallas_call | solution.py:514
  (52 shorter events, 1.4 us)
Async XLA Ops:
  0.6 28.1 %copy-start.18 = (f32[4,64]{1,0:T(4,128)S(1)}, f32[4,64]{1,0:T(4,128)}, u32[]{:S(2)}) copy-start(f32[4,64]{1,0:T(4,128)} %param.12) | copy-start | bytes 3076
  12.0 15.4 %collective-permute-start = (f32[288,128]{1,0:T(8,128)}, f32[288,128]{1,0:T(8,128)S(1)}, u32[]{:S(2)}, u32[]{:S(2)}) collective-permute-start(f32[288,128]{1,0:T(8,128)} %get-tuple-element.19), channel_id=1, source_target_pairs={{0,4},{4,8},{8,12},{12,16},{16,20},{20,24},{24,28},{1,5},{5,9},{9,... | collective-permute-start | bytes 442376 | tf_op jit(solution)/shard_map/ppermute | solution.py:19
  16.9 19.6 %collective-permute-start.1 = (f32[288,128]{1,0:T(8,128)}, f32[288,128]{1,0:T(8,128)S(1)}, u32[]{:S(2)}, u32[]{:S(2)}) collective-permute-start(f32[288,128]{1,0:T(8,128)} %get-tuple-element.20), channel_id=1, source_target_pairs={{0,8},{4,12},{8,16},{12,20},{16,24},{20,28},{1,9},{5,13},{9,17},{1... | collective-permute-start | bytes 442376 | tf_op jit(solution)/shard_map/ppermute | solution.py:19
  20.3 16.1 %collective-permute-start.2 = (f32[288,128]{1,0:T(8,128)}, f32[288,128]{1,0:T(8,128)S(1)}, u32[]{:S(2)}, u32[]{:S(2)}) collective-permute-start(f32[288,128]{1,0:T(8,128)} %get-tuple-element.21), channel_id=1, source_target_pairs={{0,12},{4,16},{8,20},{12,24},{16,28},{1,13},{5,17},{9,21},{13,25},... | collective-permute-start | bytes 442376 | tf_op jit(solution)/shard_map/ppermute | solution.py:19
  24.8 11.7 %collective-permute-start.3 = (f32[288,128]{1,0:T(8,128)}, f32[288,128]{1,0:T(8,128)S(1)}, u32[]{:S(2)}, u32[]{:S(2)}) collective-permute-start(f32[288,128]{1,0:T(8,128)} %get-tuple-element.22), channel_id=1, source_target_pairs={{4,0},{8,4},{12,8},{16,12},{20,16},{24,20},{28,24},{5,1},{9,5},{13... | collective-permute-start | bytes 442376 | tf_op jit(solution)/shard_map/ppermute | solution.py:19
  26.1 10.8 %collective-permute-start.4 = (f32[288,128]{1,0:T(8,128)}, f32[288,128]{1,0:T(8,128)S(1)}, u32[]{:S(2)}, u32[]{:S(2)}) collective-permute-start(f32[288,128]{1,0:T(8,128)} %get-tuple-element.23), channel_id=1, source_target_pairs={{8,0},{12,4},{16,8},{20,12},{24,16},{28,20},{9,1},{13,5},{17,9},{2... | collective-permute-start | bytes 442376 | tf_op jit(solution)/shard_map/ppermute | solution.py:19
  27.4 9.0 %copy-start.12 = (f32[288,128]{1,0:T(8,128)}, f32[288,128]{1,0:T(8,128)S(1)}, u32[]{:S(2)}) copy-start(f32[288,128]{1,0:T(8,128)S(1)} %collective-permute-done.refs_0_) | copy-start | bytes 442372
  27.4 10.9 %collective-permute-start.5 = (f32[288,128]{1,0:T(8,128)}, f32[288,128]{1,0:T(8,128)S(1)}, u32[]{:S(2)}, u32[]{:S(2)}) collective-permute-start(f32[288,128]{1,0:T(8,128)} %get-tuple-element.24), channel_id=1, source_target_pairs={{12,0},{16,4},{20,8},{24,12},{28,16},{13,1},{17,5},{21,9},{25,13},... | collective-permute-start | bytes 442376 | tf_op jit(solution)/shard_map/ppermute | solution.py:19
  36.4 1.9 %copy-start.13 = (f32[288,128]{1,0:T(8,128)}, f32[288,128]{1,0:T(8,128)S(1)}, u32[]{:S(2)}) copy-start(f32[288,128]{1,0:T(8,128)S(1)} %collective-permute-done.1.refs_1_) | copy-start | bytes 442372
  36.5 1.8 %copy-start.14 = (f32[288,128]{1,0:T(8,128)}, f32[288,128]{1,0:T(8,128)S(1)}, u32[]{:S(2)}) copy-start(f32[288,128]{1,0:T(8,128)S(1)} %collective-permute-done.2.refs_2_) | copy-start | bytes 442372
  36.5 1.8 %copy-start.15 = (f32[288,128]{1,0:T(8,128)}, f32[288,128]{1,0:T(8,128)S(1)}, u32[]{:S(2)}) copy-start(f32[288,128]{1,0:T(8,128)S(1)} %collective-permute-done.3.refs_3_) | copy-start | bytes 442372
  41.3 7.1 %collective-permute-start.7 = (bf16[576,256]{1,0:T(8,128)(2,1)}, bf16[576,256]{1,0:T(8,128)(2,1)S(1)}, u32[]{:S(2)}, u32[]{:S(2)}) collective-permute-start(bf16[576,256]{1,0:T(8,128)(2,1)} %activations.1.a0), channel_id=1, source_target_pairs={{0,2},{1,3},{2,0},{3,1},{4,6},{5,7},{6,4},{7,5},{8,10},{9,11},{10,... | collective-permute-start | bytes 884744 | tf_op jit(solution)/shard_map/ppermute | solution.py:525
  42.8 5.6 %collective-permute-start.6 = (bf16[576,256]{1,0:T(8,128)(2,1)}, bf16[576,256]{1,0:T(8,128)(2,1)S(1)}, u32[]{:S(2)}, u32[]{:S(2)}) collective-permute-start(bf16[576,256]{1,0:T(8,128)(2,1)} %activations.1.a0), channel_id=1, source_target_pairs={{0,1},{1,0},{2,3},{3,2},{4,5},{5,4},{6,7},{7,6},{8,9},{9,8},{10,11... | collective-permute-start | bytes 884744 | tf_op jit(solution)/shard_map/ppermute | solution.py:525
  48.4 1.6 %copy-start.3 = (bf16[576,256]{1,0:T(8,128)(2,1)}, bf16[576,256]{1,0:T(8,128)(2,1)S(1)}, u32[]{:S(2)}) copy-start(bf16[576,256]{1,0:T(8,128)(2,1)S(1)} %collective-permute-done.7.a2) | copy-start | bytes 884740
  48.4 1.6 %collective-permute-start.8 = (bf16[576,256]{1,0:T(8,128)(2,1)S(1)}, bf16[576,256]{1,0:T(8,128)(2,1)S(1)}, u32[]{:S(2)}, u32[]{:S(2)}) collective-permute-start(bf16[576,256]{1,0:T(8,128)(2,1)S(1)} %collective-permute-done.7.a2), channel_id=1, source_target_pairs={{0,1},{1,0},{2,3},{3,2},{4,5},{5,4},{6,7},{7,6},{8,9},{9,8},{10,11... | collective-permute-start | bytes 884744 | tf_op jit(solution)/shard_map/ppermute | solution.py:525
  48.4 1.6 %copy-start.4 = (bf16[576,256]{1,0:T(8,128)(2,1)}, bf16[576,256]{1,0:T(8,128)(2,1)S(1)}, u32[]{:S(2)}) copy-start(bf16[576,256]{1,0:T(8,128)(2,1)S(1)} %collective-permute-done.6.a1) | copy-start | bytes 884740
  54.4 20.9 %collective-permute-start.10 = (bf16[288,128]{1,0:T(8,128)(2,1)}, bf16[288,128]{1,0:T(8,128)(2,1)S(1)}, u32[]{:S(2)}, u32[]{:S(2)}) collective-permute-start(bf16[288,128]{1,0:T(8,128)(2,1)} %get-tuple-element.28), channel_id=1, source_target_pairs={{8,0},{12,4},{16,8},{20,12},{24,16},{28,20},{9,1},{13,5},{17,9},{2... | collective-permute-start | bytes 221192 | tf_op jit(solution)/shard_map/ppermute | solution.py:19
  55.7 21.9 %collective-permute-start.13 = (bf16[288,128]{1,0:T(8,128)(2,1)}, bf16[288,128]{1,0:T(8,128)(2,1)S(1)}, u32[]{:S(2)}, u32[]{:S(2)}) collective-permute-start(bf16[288,128]{1,0:T(8,128)(2,1)} %get-tuple-element.28), channel_id=1, source_target_pairs={{0,8},{4,12},{8,16},{12,20},{16,24},{20,28},{1,9},{5,13},{9,17},{1... | collective-permute-start | bytes 221192 | tf_op jit(solution)/shard_map/ppermute | solution.py:19
  62.1 15.3 %collective-permute-start.11 = (bf16[288,128]{1,0:T(8,128)(2,1)}, bf16[288,128]{1,0:T(8,128)(2,1)S(1)}, u32[]{:S(2)}, u32[]{:S(2)}) collective-permute-start(bf16[288,128]{1,0:T(8,128)(2,1)} %get-tuple-element.29), channel_id=1, source_target_pairs={{12,0},{16,4},{20,8},{24,12},{28,16},{13,1},{17,5},{21,9},{25,13},... | collective-permute-start | bytes 221192 | tf_op jit(solution)/shard_map/ppermute | solution.py:19
  63.4 14.2 %collective-permute-start.14 = (bf16[288,128]{1,0:T(8,128)(2,1)}, bf16[288,128]{1,0:T(8,128)(2,1)S(1)}, u32[]{:S(2)}, u32[]{:S(2)}) collective-permute-start(bf16[288,128]{1,0:T(8,128)(2,1)} %get-tuple-element.29), channel_id=1, source_target_pairs={{0,12},{4,16},{8,20},{12,24},{16,28},{1,13},{5,17},{9,21},{13,25},... | collective-permute-start | bytes 221192 | tf_op jit(solution)/shard_map/ppermute | solution.py:19
  69.2 8.3 %collective-permute-start.12 = (bf16[288,128]{1,0:T(8,128)(2,1)}, bf16[288,128]{1,0:T(8,128)(2,1)S(1)}, u32[]{:S(2)}, u32[]{:S(2)}) collective-permute-start(bf16[288,128]{1,0:T(8,128)(2,1)} %get-tuple-element.27), channel_id=1, source_target_pairs={{0,4},{4,8},{8,12},{12,16},{16,20},{20,24},{24,28},{1,5},{5,9},{9,... | collective-permute-start | bytes 221192 | tf_op jit(solution)/shard_map/ppermute | solution.py:19
  75.3 6.5 %copy-start.6 = (bf16[288,128]{1,0:T(8,128)(2,1)}, bf16[288,128]{1,0:T(8,128)(2,1)S(1)}, u32[]{:S(2)}) copy-start(bf16[288,128]{1,0:T(8,128)(2,1)S(1)} %collective-permute-done.10.refs_1_) | copy-start | bytes 221188
  75.3 6.5 %collective-permute-start.9 = (bf16[288,128]{1,0:T(8,128)(2,1)}, bf16[288,128]{1,0:T(8,128)(2,1)S(1)}, u32[]{:S(2)}, u32[]{:S(2)}) collective-permute-start(bf16[288,128]{1,0:T(8,128)(2,1)} %get-tuple-element.27), channel_id=1, source_target_pairs={{4,0},{8,4},{12,8},{16,12},{20,16},{24,20},{28,24},{5,1},{9,5},{13... | collective-permute-start | bytes 221192 | tf_op jit(solution)/shard_map/ppermute | solution.py:19
  77.5 4.3 %copy-start.8 = (bf16[288,128]{1,0:T(8,128)(2,1)}, bf16[288,128]{1,0:T(8,128)(2,1)S(1)}, u32[]{:S(2)}) copy-start(bf16[288,128]{1,0:T(8,128)(2,1)S(1)} %collective-permute-done.11.refs_2_) | copy-start | bytes 221188
  77.6 4.2 %copy-start.10 = (bf16[288,128]{1,0:T(8,128)(2,1)}, bf16[288,128]{1,0:T(8,128)(2,1)S(1)}, u32[]{:S(2)}) copy-start(bf16[288,128]{1,0:T(8,128)(2,1)S(1)} %collective-permute-done.12.refs_3_) | copy-start | bytes 221188
  77.6 4.2 %copy-start.7 = (bf16[288,128]{1,0:T(8,128)(2,1)}, bf16[288,128]{1,0:T(8,128)(2,1)S(1)}, u32[]{:S(2)}) copy-start(bf16[288,128]{1,0:T(8,128)(2,1)S(1)} %collective-permute-done.13.refs_4_) | copy-start | bytes 221188
  77.6 4.2 %copy-start.9 = (bf16[288,128]{1,0:T(8,128)(2,1)}, bf16[288,128]{1,0:T(8,128)(2,1)S(1)}, u32[]{:S(2)}) copy-start(bf16[288,128]{1,0:T(8,128)(2,1)S(1)} %collective-permute-done.14.refs_5_) | copy-start | bytes 221188
  89.2 7.5 %collective-permute-start.16 = (bf16[576,512]{1,0:T(8,128)(2,1)}, bf16[576,512]{1,0:T(8,128)(2,1)S(1)}, u32[]{:S(2)}, u32[]{:S(2)}) collective-permute-start(bf16[576,512]{1,0:T(8,128)(2,1)} %get-tuple-element.32), channel_id=1, source_target_pairs={{0,1},{1,0},{2,3},{3,2},{4,5},{5,4},{6,7},{7,6},{8,9},{9,8},{10,11... | collective-permute-start | bytes 1769480 | tf_op jit(solution)/shard_map/ppermute | solution.py:525
  89.3 7.4 %copy-start = (bf16[576,512]{1,0:T(8,128)(2,1)S(1)}, bf16[576,512]{1,0:T(8,128)(2,1)}, u32[]{:S(2)}) copy-start(bf16[576,512]{1,0:T(8,128)(2,1)} %get-tuple-element.33) | copy-start | bytes 1769476
  96.2 2.4 %collective-permute-start.15 = (bf16[576,512]{1,0:T(8,128)(2,1)}, bf16[576,512]{1,0:T(8,128)(2,1)S(1)}, u32[]{:S(2)}, u32[]{:S(2)}) collective-permute-start(bf16[576,512]{1,0:T(8,128)(2,1)} %get-tuple-element.31), channel_id=1, source_target_pairs={{0,1},{1,0},{2,3},{3,2},{4,5},{5,4},{6,7},{7,6},{8,9},{9,8},{10,11... | collective-permute-start | bytes 1769480 | tf_op jit(solution)/shard_map/ppermute | solution.py:525
  96.9 15.3 %collective-permute-start.17 = (bf16[576,512]{1,0:T(8,128)(2,1)S(1)}, bf16[576,512]{1,0:T(8,128)(2,1)S(1)}, u32[]{:S(2)}, u32[]{:S(2)}) collective-permute-start(bf16[576,512]{1,0:T(8,128)(2,1)S(1)} %add_convert_fusion), channel_id=1, source_target_pairs={{0,2},{1,3},{2,0},{3,1},{4,6},{5,7},{6,4},{7,5},{8,10},{9,11},{10,... | collective-permute-start | bytes 1769480 | tf_op jit(solution)/shard_map/ppermute | solution.py:525
  98.6 13.7 %copy-start.1 = (bf16[576,512]{1,0:T(8,128)(2,1)}, bf16[576,512]{1,0:T(8,128)(2,1)S(1)}, u32[]{:S(2)}) copy-start(bf16[576,512]{1,0:T(8,128)(2,1)S(1)} %collective-permute-done.15.b) | copy-start | bytes 1769476
  (5 other events, 4.3 us)
